TPU v7x, 512 devices: a whole 4x8x8 slice. The times are simulated.
512 devices in a mesh: video: 64 (over x, y, core), audio: 8 (over z).
Axes of the slice: x: 4, y: 8, z: 8, core: 2. Of those that a mesh axis runs over, the one named last changes fastest.
Arguments:
- video_query: bfloat16 [65536, 3072], P('video', 'audio'), may hold values from -12 to 12
- video_key: bfloat16 [65536, 3072], P('video', 'audio'), may hold values from -12 to 12
- video_value: bfloat16 [65536, 3072], P('video', 'audio'), may hold values from -6 to 6
- audio_query: bfloat16 [8192, 3072], P('video', 'audio'), may hold values from -12 to 12
- audio_key: bfloat16 [8192, 3072], P('video', 'audio'), may hold values from -12 to 12
- audio_value: bfloat16 [8192, 3072], P('video', 'audio'), may hold values from -6 to 6
- video_query_gain: float32 [3072], P('audio'), may hold values from 0.5 to 2
- video_key_gain: float32 [3072], P('audio'), may hold values from 0.5 to 2
- audio_query_gain: float32 [3072], P('audio'), may hold values from 0.5 to 2
- audio_key_gain: float32 [3072], P('audio'), may hold values from 0.5 to 2
- block_pairs: int32 [64, 16], replicated, may hold values from 0 to 511, as said below
Outputs:
- video_mixed: float32 [65536, 3072], P('video', 'audio')
- audio_mixed: float32 [8192, 3072], P('video', 'audio')
Inputs may be any that keep to these rules, and one draw needn't show every extreme that they name: `block_pairs`: each row holds 16 different video blocks; a block v named in row a satisfies |(v * 128) // 1024 - (a * 128) // 128| <= 2; every video block is named in some row.
All inputs are finite; a program needn't handle non-finite values.
Results may differ from a plain program's by a relative error of at most 0.011.
Values may be sent and summed in bfloat16 or wider, within the bound.
A program may use at most 64 MiB of HBM per device.

v0:
```python
import math

import jax
import jax.numpy as jnp
from jax import lax
from jax.sharding import PartitionSpec as P

E = 128
BLOCK = 128
REACH = 2


EPS = 1e-06
MASKED = -1e30


def shifted(value, axis, steps):
    count = lax.axis_size(axis)
    first, last = (max(0, -steps), min(count, count - steps))
    return lax.ppermute(value, axis, [(source, source + steps) for source in range(first, last)])


def block_mask(pairs, count):
    named = pairs[:, :, None] == jnp.arange(count, dtype=jnp.int32)[None, None, :]
    return jnp.any(named, axis=1)


def squares(source):
    wide = source.astype(jnp.float32)
    return jnp.sum(wide * wide, axis=1)


def normalize(source, total, gain, width):
    wide = source.astype(jnp.float32)
    return (wide * lax.rsqrt(total / width + EPS)[:, None] * gain[None, :]).astype(jnp.bfloat16)


def attend_parts(queries, key_rows, values, allowed):
    query_count = queries.shape[0]
    key_count = key_rows.shape[0]
    blended = []
    maxima = []
    totals = []
    for head_index in range(queries.shape[1] // E):
        columns = slice(head_index * E, (head_index + 1) * E)
        scores = lax.dot_general(
            queries[:, columns],
            key_rows[:, columns],
            (((1,), (1,)), ((), ())),
            preferred_element_type=jnp.float32,
        ) * (1.0 / math.sqrt(E))
        allowed_here = allowed[:, None, :, None]
        shaped = scores.reshape(query_count // BLOCK, BLOCK, key_count // BLOCK, BLOCK)
        shaped = jnp.where(allowed_here, shaped, MASKED)
        row_max = jnp.max(shaped, axis=(2, 3), keepdims=True)
        weights = jnp.where(allowed_here, jnp.exp(shaped - row_max), 0.0)
        row_total = jnp.sum(weights, axis=(2, 3)).reshape(query_count)
        rounded = weights.astype(jnp.bfloat16).reshape(query_count, key_count)
        blended.append(jnp.dot(rounded, values[:, columns], preferred_element_type=jnp.float32))
        maxima.append(row_max.reshape(query_count))
        totals.append(row_total)
    return (jnp.concatenate(blended, axis=1), jnp.stack(maxima, axis=1), jnp.stack(totals, axis=1))


def finish(blended, row_total):
    row_count, head_count = row_total.shape
    scaled = blended.reshape(row_count, head_count, E) / row_total[:, :, None]
    return scaled.reshape(row_count, head_count * E)


def body(
    video_query,
    video_key,
    video_value,
    audio_query,
    audio_key,
    audio_value,
    video_query_gain,
    video_key_gain,
    audio_query_gain,
    audio_key_gain,
    block_pairs,
):
    width = video_query.shape[1] * lax.axis_size("audio")
    sums = lax.psum(
        (squares(video_query), squares(video_key), squares(audio_query), squares(audio_key)),
        "audio",
    )
    video_queries = normalize(video_query, sums[0], video_query_gain, width)
    video_keys = normalize(video_key, sums[1], video_key_gain, width)
    audio_queries = normalize(audio_query, sums[2], audio_query_gain, width)
    audio_keys = normalize(audio_key, sums[3], audio_key_gain, width)
    device = lax.axis_index("video")
    devices = lax.axis_size("video")
    video_span = video_query.shape[0] // BLOCK
    audio_span = audio_query.shape[0] // BLOCK
    window = 2 * REACH + 1
    pairs_mask = block_mask(block_pairs, devices * video_span)
    row_padded = jnp.pad(pairs_mask, ((REACH * audio_span, REACH * audio_span), (0, 0)))
    col_padded = jnp.pad(pairs_mask, ((0, 0), (REACH * video_span, REACH * video_span)))
    audio_near = []
    for offset in range(-REACH, REACH + 1):
        if offset == 0:
            audio_near.append((audio_keys, audio_value))
        else:
            audio_near.append(shifted((audio_keys, audio_value), "video", -offset))
    near_keys = jnp.concatenate([piece[0] for piece in audio_near], axis=0)
    near_values = jnp.concatenate([piece[1] for piece in audio_near], axis=0)
    video_allowed = lax.dynamic_slice(
        row_padded, (device * audio_span, device * video_span), (window * audio_span, video_span)
    ).T
    blended, maxima, totals = attend_parts(video_queries, near_keys, near_values, video_allowed)
    video_mixed = finish(blended, totals)
    video_near = []
    for offset in range(-REACH, REACH + 1):
        if offset == 0:
            video_near.append((video_keys, video_value))
        else:
            video_near.append(shifted((video_keys, video_value), "video", -offset))
    far_keys = jnp.concatenate([piece[0] for piece in video_near], axis=0)
    far_values = jnp.concatenate([piece[1] for piece in video_near], axis=0)
    audio_allowed = lax.dynamic_slice(
        col_padded, (device * audio_span, device * video_span), (audio_span, window * video_span)
    )
    blended, maxima, totals = attend_parts(audio_queries, far_keys, far_values, audio_allowed)
    audio_mixed = finish(blended, totals)
    return (video_mixed, audio_mixed)


def solution(mesh):
    placed = (
        P("video", "audio"),
        P("video", "audio"),
        P("video", "audio"),
        P("video", "audio"),
        P("video", "audio"),
        P("video", "audio"),
        P("audio"),
        P("audio"),
        P("audio"),
        P("audio"),
        P(),
    )
    return jax.shard_map(
        body,
        mesh=mesh,
        in_specs=placed,
        out_specs=(P("video", "audio"), P("video", "audio")),
        check_vma=False,
    )
```

profile of v0, /device:TPU:6, one launch (start us, length us, event | category | flops | bytes accessed | tf_op | source)
XLA Modules:
  0.0 163.0 jit_solution(7713336753472520714)
XLA Ops:
  3.6 23.7 %all-reduce.2 = (f32[1024]{0:T(1024)S(1)}, f32[128]{0:T(128)S(1)}, f32[1024]{0:T(1024)S(1)}, f32[128]{0:T(128)S(1)}) all-reduce(f32[1024]{0:T(1024)S(1)} %get-tuple-element.27, f32[128]{0:T(128)S(1)} %get-tuple-element.29, f32[1024]{0:T(1024)S(1)} %get-tuple-element.28, ...), channel_id=1, replica_groups=mesh['video'=64,'audio'=8] {'audio'}, use_global_device_ids=true, to_apply=%region_2.0 | all-reduce | flops 2304 | bytes 18432 | tf_op jit(solution)/shard_map/psum | solution.py:85
  28.7 3.5 %collective-permute-start.8 = (bf16[1024,384]{1,0:T(8,128)(2,1)S(1)}, bf16[1024,384]{1,0:T(8,128)(2,1)}, u32[]{:S(2)}, u32[]{:S(2)}) collective-permute-start(bf16[1024,384]{1,0:T(8,128)(2,1)S(1)} %fusion.18), channel_id=1, source_target_pairs={{0,16},{8,24},{16,32},{24,40},{32,48},{40,56},{48,64},{56,72},{64,... | collective-permute-start | bytes 2359304 | tf_op jit(solution)/shard_map/ppermute | solution.py:20
  32.2 1.9 %collective-permute-start.9 = (bf16[1024,384]{1,0:T(8,128)(2,1)S(1)}, bf16[1024,384]{1,0:T(8,128)(2,1)}, u32[]{:S(2)}, u32[]{:S(2)}) collective-permute-start(bf16[1024,384]{1,0:T(8,128)(2,1)S(1)} %fusion.18), channel_id=1, source_target_pairs={{0,8},{8,16},{16,24},{24,32},{32,40},{40,48},{48,56},{56,64},{64,7... | collective-permute-start | bytes 2359304 | tf_op jit(solution)/shard_map/ppermute | solution.py:20
  34.2 5.8 %collective-permute-start.10 = (bf16[1024,384]{1,0:T(8,128)(2,1)S(1)}, bf16[1024,384]{1,0:T(8,128)(2,1)}, u32[]{:S(2)}, u32[]{:S(2)}) collective-permute-start(bf16[1024,384]{1,0:T(8,128)(2,1)S(1)} %fusion.18), channel_id=1, source_target_pairs={{8,0},{16,8},{24,16},{32,24},{40,32},{48,40},{56,48},{64,56},{72,6... | collective-permute-start | bytes 2359304 | tf_op jit(solution)/shard_map/ppermute | solution.py:20
  39.9 2.4 %collective-permute-start.11 = (bf16[1024,384]{1,0:T(8,128)(2,1)S(1)}, bf16[1024,384]{1,0:T(8,128)(2,1)}, u32[]{:S(2)}, u32[]{:S(2)}) collective-permute-start(bf16[1024,384]{1,0:T(8,128)(2,1)S(1)} %fusion.18), channel_id=1, source_target_pairs={{16,0},{24,8},{32,16},{40,24},{48,32},{56,40},{64,48},{72,56},{80,... | collective-permute-start | bytes 2359304 | tf_op jit(solution)/shard_map/ppermute | solution.py:20
  42.4 3.5 %collective-permute-start = (bf16[128,384]{1,0:T(8,128)(2,1)S(1)}, bf16[128,384]{1,0:T(8,128)(2,1)S(1)}, u32[]{:S(2)}, u32[]{:S(2)}) collective-permute-start(bf16[128,384]{1,0:T(8,128)(2,1)S(1)} %fusion.60), channel_id=1, source_target_pairs={{0,16},{8,24},{16,32},{24,40},{32,48},{40,56},{48,64},{56,72},{64,... | collective-permute-start | bytes 294920 | tf_op jit(solution)/shard_map/ppermute | solution.py:20
  47.2 8.1 %collective-permute-done = bf16[128,384]{1,0:T(8,128)(2,1)S(1)} collective-permute-done((bf16[128,384]{1,0:T(8,128)(2,1)S(1)}, bf16[128,384]{1,0:T(8,128)(2,1)S(1)}, u32[]{:S(2)}, u32[]{:S(2)}) %collective-permute-start) | collective-permute-done | bytes 98336 | tf_op jit(solution)/shard_map/ppermute | solution.py:20
  55.3 5.2 %collective-permute-start.1 = (bf16[128,384]{1,0:T(8,128)(2,1)S(1)}, bf16[128,384]{1,0:T(8,128)(2,1)S(1)}, u32[]{:S(2)}, u32[]{:S(2)}) collective-permute-start(bf16[128,384]{1,0:T(8,128)(2,1)S(1)} %fusion.60), channel_id=1, source_target_pairs={{0,8},{8,16},{16,24},{24,32},{32,40},{40,48},{48,56},{56,64},{64,7... | collective-permute-start | bytes 294920 | tf_op jit(solution)/shard_map/ppermute | solution.py:20
  60.5 3.5 %collective-permute-done.1 = bf16[128,384]{1,0:T(8,128)(2,1)S(1)} collective-permute-done((bf16[128,384]{1,0:T(8,128)(2,1)S(1)}, bf16[128,384]{1,0:T(8,128)(2,1)S(1)}, u32[]{:S(2)}, u32[]{:S(2)}) %collective-permute-start.1) | collective-permute-done | bytes 98336 | tf_op jit(solution)/shard_map/ppermute | solution.py:20
  64.0 1.9 %collective-permute-start.2 = (bf16[128,384]{1,0:T(8,128)(2,1)S(1)}, bf16[128,384]{1,0:T(8,128)(2,1)S(1)}, u32[]{:S(2)}, u32[]{:S(2)}) collective-permute-start(bf16[128,384]{1,0:T(8,128)(2,1)S(1)} %fusion.60), channel_id=1, source_target_pairs={{8,0},{16,8},{24,16},{32,24},{40,32},{48,40},{56,48},{64,56},{72,6... | collective-permute-start | bytes 294920 | tf_op jit(solution)/shard_map/ppermute | solution.py:20
  66.1 2.1 %collective-permute-done.2 = bf16[128,384]{1,0:T(8,128)(2,1)S(1)} collective-permute-done((bf16[128,384]{1,0:T(8,128)(2,1)S(1)}, bf16[128,384]{1,0:T(8,128)(2,1)S(1)}, u32[]{:S(2)}, u32[]{:S(2)}) %collective-permute-start.2) | collective-permute-done | bytes 98336 | tf_op jit(solution)/shard_map/ppermute | solution.py:20
  68.1 3.6 %collective-permute-start.3 = (bf16[128,384]{1,0:T(8,128)(2,1)S(1)}, bf16[128,384]{1,0:T(8,128)(2,1)S(1)}, u32[]{:S(2)}, u32[]{:S(2)}) collective-permute-start(bf16[128,384]{1,0:T(8,128)(2,1)S(1)} %fusion.60), channel_id=1, source_target_pairs={{16,0},{24,8},{32,16},{40,24},{48,32},{56,40},{64,48},{72,56},{80,... | collective-permute-start | bytes 294920 | tf_op jit(solution)/shard_map/ppermute | solution.py:20
  71.8 3.5 %collective-permute-done.3 = bf16[128,384]{1,0:T(8,128)(2,1)S(1)} collective-permute-done((bf16[128,384]{1,0:T(8,128)(2,1)S(1)}, bf16[128,384]{1,0:T(8,128)(2,1)S(1)}, u32[]{:S(2)}, u32[]{:S(2)}) %collective-permute-start.3) | collective-permute-done | bytes 98336 | tf_op jit(solution)/shard_map/ppermute | solution.py:20
  75.3 2.5 %collective-permute-start.4 = (bf16[128,384]{1,0:T(8,128)(2,1)S(1)}, bf16[128,384]{1,0:T(8,128)(2,1)S(1)}, u32[]{:S(2)}, u32[]{:S(2)}) collective-permute-start(bf16[128,384]{1,0:T(8,128)(2,1)S(1)} %copy-done.5), channel_id=1, source_target_pairs={{0,16},{8,24},{16,32},{24,40},{32,48},{40,56},{48,64},{56,72},{64,... | collective-permute-start | bytes 294920 | tf_op jit(solution)/shard_map/ppermute | solution.py:20
  81.0 3.8 %collective-permute-done.4 = bf16[128,384]{1,0:T(8,128)(2,1)S(1)} collective-permute-done((bf16[128,384]{1,0:T(8,128)(2,1)S(1)}, bf16[128,384]{1,0:T(8,128)(2,1)S(1)}, u32[]{:S(2)}, u32[]{:S(2)}) %collective-permute-start.4) | collective-permute-done | bytes 98336 | tf_op jit(solution)/shard_map/ppermute | solution.py:20
  86.7 6.1 %collective-permute-done.5 = bf16[128,384]{1,0:T(8,128)(2,1)S(1)} collective-permute-done((bf16[128,384]{1,0:T(8,128)(2,1)S(1)}, bf16[128,384]{1,0:T(8,128)(2,1)S(1)}, u32[]{:S(2)}, u32[]{:S(2)}) %collective-permute-start.5) | collective-permute-done | bytes 98336 | tf_op jit(solution)/shard_map/ppermute | solution.py:20
  94.8 2.1 %collective-permute-done.6 = bf16[128,384]{1,0:T(8,128)(2,1)S(1)} collective-permute-done((bf16[128,384]{1,0:T(8,128)(2,1)S(1)}, bf16[128,384]{1,0:T(8,128)(2,1)S(1)}, u32[]{:S(2)}, u32[]{:S(2)}) %collective-permute-start.6) | collective-permute-done | bytes 98336 | tf_op jit(solution)/shard_map/ppermute | solution.py:20
  98.9 4.6 %collective-permute-done.7 = bf16[128,384]{1,0:T(8,128)(2,1)S(1)} collective-permute-done((bf16[128,384]{1,0:T(8,128)(2,1)S(1)}, bf16[128,384]{1,0:T(8,128)(2,1)S(1)}, u32[]{:S(2)}, u32[]{:S(2)}) %collective-permute-start.7) | collective-permute-done | bytes 98336 | tf_op jit(solution)/shard_map/ppermute | solution.py:20
  103.4 1.9 %collective-permute-start.12 = (bf16[1024,384]{1,0:T(8,128)(2,1)S(1)}, bf16[1024,384]{1,0:T(8,128)(2,1)}, u32[]{:S(2)}, u32[]{:S(2)}) collective-permute-start(bf16[1024,384]{1,0:T(8,128)(2,1)S(1)} %copy-done.3), channel_id=1, source_target_pairs={{0,16},{8,24},{16,32},{24,40},{32,48},{40,56},{48,64},{56,72},{64,... | collective-permute-start | bytes 2359304 | tf_op jit(solution)/shard_map/ppermute | solution.py:20
  111.4 3.1 %collective-permute-start.13 = (bf16[1024,384]{1,0:T(8,128)(2,1)S(1)}, bf16[1024,384]{1,0:T(8,128)(2,1)S(1)}, u32[]{:S(2)}, u32[]{:S(2)}) collective-permute-start(bf16[1024,384]{1,0:T(8,128)(2,1)S(1)} %copy-done.3), channel_id=1, source_target_pairs={{0,8},{8,16},{16,24},{24,32},{32,40},{40,48},{48,56},{56,64},{64,7... | collective-permute-start | bytes 2359304 | tf_op jit(solution)/shard_map/ppermute | solution.py:20
  115.8 11.8 %collective-permute-done.12 = bf16[1024,384]{1,0:T(8,128)(2,1)} collective-permute-done((bf16[1024,384]{1,0:T(8,128)(2,1)S(1)}, bf16[1024,384]{1,0:T(8,128)(2,1)}, u32[]{:S(2)}, u32[]{:S(2)}) %collective-permute-start.12) | collective-permute-done | bytes 786464 | tf_op jit(solution)/shard_map/ppermute | solution.py:20
  130.7 2.1 %collective-permute-start.15 = (bf16[1024,384]{1,0:T(8,128)(2,1)S(1)}, bf16[1024,384]{1,0:T(8,128)(2,1)S(1)}, u32[]{:S(2)}, u32[]{:S(2)}) collective-permute-start(bf16[1024,384]{1,0:T(8,128)(2,1)S(1)} %copy-done.3), channel_id=1, source_target_pairs={{16,0},{24,8},{32,16},{40,24},{48,32},{56,40},{64,48},{72,56},{80,... | collective-permute-start | bytes 2359304 | tf_op jit(solution)/shard_map/ppermute | solution.py:20
  138.0 6.3 %collective-permute-done.14 = bf16[1024,384]{1,0:T(8,128)(2,1)S(1)} collective-permute-done((bf16[1024,384]{1,0:T(8,128)(2,1)S(1)}, bf16[1024,384]{1,0:T(8,128)(2,1)S(1)}, u32[]{:S(2)}, u32[]{:S(2)}) %collective-permute-start.14) | collective-permute-done | bytes 786464 | tf_op jit(solution)/shard_map/ppermute | solution.py:20
  145.8 12.3 %collective-permute-done.15 = bf16[1024,384]{1,0:T(8,128)(2,1)S(1)} collective-permute-done((bf16[1024,384]{1,0:T(8,128)(2,1)S(1)}, bf16[1024,384]{1,0:T(8,128)(2,1)S(1)}, u32[]{:S(2)}, u32[]{:S(2)}) %collective-permute-start.15) | collective-permute-done | bytes 786464 | tf_op jit(solution)/shard_map/ppermute | solution.py:20
  (87 shorter events, 36.5 us)
Async XLA Ops:
  0.6 46.2 %copy-start.1 = (bf16[1024,384]{1,0:T(8,128)(2,1)S(1)}, bf16[1024,384]{1,0:T(8,128)(2,1)}, u32[]{:S(2)}) copy-start(bf16[1024,384]{1,0:T(8,128)(2,1)} %param.11) | copy-start | bytes 2359300
  0.6 46.1 %copy-start.4 = (bf16[128,384]{1,0:T(8,128)(2,1)S(1)}, bf16[128,384]{1,0:T(8,128)(2,1)}, u32[]{:S(2)}) copy-start(bf16[128,384]{1,0:T(8,128)(2,1)} %param.14) | copy-start | bytes 294916
  0.7 41.6 %copy-start.2 = (bf16[128,384]{1,0:T(8,128)(2,1)S(1)}, bf16[128,384]{1,0:T(8,128)(2,1)}, u32[]{:S(2)}) copy-start(bf16[128,384]{1,0:T(8,128)(2,1)} %param.15) | copy-start | bytes 294916
  0.7 41.6 %copy-start.6 = (f32[384]{0:T(512)S(1)}, f32[384]{0:T(512)}, u32[]{:S(2)}) copy-start(f32[384]{0:T(512)} %param.20) | copy-start | bytes 4612
  0.7 45.2 %copy-start.8 = (s32[64,16]{0,1:T(8,128)S(1)}, s32[64,16]{0,1:T(8,128)}, u32[]{:S(2)}) copy-start(s32[64,16]{0,1:T(8,128)} %param.21) | copy-start | bytes 12292
  0.7 46.1 %copy-start.9 = (f32[384]{0:T(512)S(1)}, f32[384]{0:T(512)}, u32[]{:S(2)}) copy-start(f32[384]{0:T(512)} %param.19) | copy-start | bytes 4612
  0.7 46.2 %copy-start.10 = (f32[384]{0:T(512)S(1)}, f32[384]{0:T(512)}, u32[]{:S(2)}) copy-start(f32[384]{0:T(512)} %param.17) | copy-start | bytes 4612
  2.5 72.8 %copy-start.5 = (bf16[128,384]{1,0:T(8,128)(2,1)S(1)}, bf16[128,384]{1,0:T(8,128)(2,1)}, u32[]{:S(2)}) copy-start(bf16[128,384]{1,0:T(8,128)(2,1)} %param.16) | copy-start | bytes 294916
  28.7 82.7 %collective-permute-start.8 = (bf16[1024,384]{1,0:T(8,128)(2,1)S(1)}, bf16[1024,384]{1,0:T(8,128)(2,1)}, u32[]{:S(2)}, u32[]{:S(2)}) collective-permute-start(bf16[1024,384]{1,0:T(8,128)(2,1)S(1)} %fusion.18), channel_id=1, source_target_pairs={{0,16},{8,24},{16,32},{24,40},{32,48},{40,56},{48,64},{56,72},{64,... | collective-permute-start | bytes 2359304 | tf_op jit(solution)/shard_map/ppermute | solution.py:20
  32.2 98.5 %collective-permute-start.9 = (bf16[1024,384]{1,0:T(8,128)(2,1)S(1)}, bf16[1024,384]{1,0:T(8,128)(2,1)}, u32[]{:S(2)}, u32[]{:S(2)}) collective-permute-start(bf16[1024,384]{1,0:T(8,128)(2,1)S(1)} %fusion.18), channel_id=1, source_target_pairs={{0,8},{8,16},{16,24},{24,32},{32,40},{40,48},{48,56},{56,64},{64,7... | collective-permute-start | bytes 2359304 | tf_op jit(solution)/shard_map/ppermute | solution.py:20
  34.2 100.3 %collective-permute-start.10 = (bf16[1024,384]{1,0:T(8,128)(2,1)S(1)}, bf16[1024,384]{1,0:T(8,128)(2,1)}, u32[]{:S(2)}, u32[]{:S(2)}) collective-permute-start(bf16[1024,384]{1,0:T(8,128)(2,1)S(1)} %fusion.18), channel_id=1, source_target_pairs={{8,0},{16,8},{24,16},{32,24},{40,32},{48,40},{56,48},{64,56},{72,6... | collective-permute-start | bytes 2359304 | tf_op jit(solution)/shard_map/ppermute | solution.py:20
  39.9 95.8 %collective-permute-start.11 = (bf16[1024,384]{1,0:T(8,128)(2,1)S(1)}, bf16[1024,384]{1,0:T(8,128)(2,1)}, u32[]{:S(2)}, u32[]{:S(2)}) collective-permute-start(bf16[1024,384]{1,0:T(8,128)(2,1)S(1)} %fusion.18), channel_id=1, source_target_pairs={{16,0},{24,8},{32,16},{40,24},{48,32},{56,40},{64,48},{72,56},{80,... | collective-permute-start | bytes 2359304 | tf_op jit(solution)/shard_map/ppermute | solution.py:20
  42.4 12.9 %collective-permute-start = (bf16[128,384]{1,0:T(8,128)(2,1)S(1)}, bf16[128,384]{1,0:T(8,128)(2,1)S(1)}, u32[]{:S(2)}, u32[]{:S(2)}) collective-permute-start(bf16[128,384]{1,0:T(8,128)(2,1)S(1)} %fusion.60), channel_id=1, source_target_pairs={{0,16},{8,24},{16,32},{24,40},{32,48},{40,56},{48,64},{56,72},{64,... | collective-permute-start | bytes 294920 | tf_op jit(solution)/shard_map/ppermute | solution.py:20
  55.3 8.7 %collective-permute-start.1 = (bf16[128,384]{1,0:T(8,128)(2,1)S(1)}, bf16[128,384]{1,0:T(8,128)(2,1)S(1)}, u32[]{:S(2)}, u32[]{:S(2)}) collective-permute-start(bf16[128,384]{1,0:T(8,128)(2,1)S(1)} %fusion.60), channel_id=1, source_target_pairs={{0,8},{8,16},{16,24},{24,32},{32,40},{40,48},{48,56},{56,64},{64,7... | collective-permute-start | bytes 294920 | tf_op jit(solution)/shard_map/ppermute | solution.py:20
  64.0 4.1 %collective-permute-start.2 = (bf16[128,384]{1,0:T(8,128)(2,1)S(1)}, bf16[128,384]{1,0:T(8,128)(2,1)S(1)}, u32[]{:S(2)}, u32[]{:S(2)}) collective-permute-start(bf16[128,384]{1,0:T(8,128)(2,1)S(1)} %fusion.60), channel_id=1, source_target_pairs={{8,0},{16,8},{24,16},{32,24},{40,32},{48,40},{56,48},{64,56},{72,6... | collective-permute-start | bytes 294920 | tf_op jit(solution)/shard_map/ppermute | solution.py:20
  68.1 7.2 %collective-permute-start.3 = (bf16[128,384]{1,0:T(8,128)(2,1)S(1)}, bf16[128,384]{1,0:T(8,128)(2,1)S(1)}, u32[]{:S(2)}, u32[]{:S(2)}) collective-permute-start(bf16[128,384]{1,0:T(8,128)(2,1)S(1)} %fusion.60), channel_id=1, source_target_pairs={{16,0},{24,8},{32,16},{40,24},{48,32},{56,40},{64,48},{72,56},{80,... | collective-permute-start | bytes 294920 | tf_op jit(solution)/shard_map/ppermute | solution.py:20
  75.3 9.5 %collective-permute-start.4 = (bf16[128,384]{1,0:T(8,128)(2,1)S(1)}, bf16[128,384]{1,0:T(8,128)(2,1)S(1)}, u32[]{:S(2)}, u32[]{:S(2)}) collective-permute-start(bf16[128,384]{1,0:T(8,128)(2,1)S(1)} %copy-done.5), channel_id=1, source_target_pairs={{0,16},{8,24},{16,32},{24,40},{32,48},{40,56},{48,64},{56,72},{64,... | collective-permute-start | bytes 294920 | tf_op jit(solution)/shard_map/ppermute | solution.py:20
  84.8 8.0 %collective-permute-start.5 = (bf16[128,384]{1,0:T(8,128)(2,1)S(1)}, bf16[128,384]{1,0:T(8,128)(2,1)S(1)}, u32[]{:S(2)}, u32[]{:S(2)}) collective-permute-start(bf16[128,384]{1,0:T(8,128)(2,1)S(1)} %copy-done.5), channel_id=1, source_target_pairs={{0,8},{8,16},{16,24},{24,32},{32,40},{40,48},{48,56},{56,64},{64,7... | collective-permute-start | bytes 294920 | tf_op jit(solution)/shard_map/ppermute | solution.py:20
  92.8 4.1 %collective-permute-start.6 = (bf16[128,384]{1,0:T(8,128)(2,1)S(1)}, bf16[128,384]{1,0:T(8,128)(2,1)S(1)}, u32[]{:S(2)}, u32[]{:S(2)}) collective-permute-start(bf16[128,384]{1,0:T(8,128)(2,1)S(1)} %copy-done.5), channel_id=1, source_target_pairs={{8,0},{16,8},{24,16},{32,24},{40,32},{48,40},{56,48},{64,56},{72,6... | collective-permute-start | bytes 294920 | tf_op jit(solution)/shard_map/ppermute | solution.py:20
  96.9 6.5 %collective-permute-start.7 = (bf16[128,384]{1,0:T(8,128)(2,1)S(1)}, bf16[128,384]{1,0:T(8,128)(2,1)S(1)}, u32[]{:S(2)}, u32[]{:S(2)}) collective-permute-start(bf16[128,384]{1,0:T(8,128)(2,1)S(1)} %copy-done.5), channel_id=1, source_target_pairs={{16,0},{24,8},{32,16},{40,24},{48,32},{56,40},{64,48},{72,56},{80,... | collective-permute-start | bytes 294920 | tf_op jit(solution)/shard_map/ppermute | solution.py:20
  103.4 24.1 %collective-permute-start.12 = (bf16[1024,384]{1,0:T(8,128)(2,1)S(1)}, bf16[1024,384]{1,0:T(8,128)(2,1)}, u32[]{:S(2)}, u32[]{:S(2)}) collective-permute-start(bf16[1024,384]{1,0:T(8,128)(2,1)S(1)} %copy-done.3), channel_id=1, source_target_pairs={{0,16},{8,24},{16,32},{24,40},{32,48},{40,56},{48,64},{56,72},{64,... | collective-permute-start | bytes 2359304 | tf_op jit(solution)/shard_map/ppermute | solution.py:20
  111.4 25.6 %collective-permute-start.13 = (bf16[1024,384]{1,0:T(8,128)(2,1)S(1)}, bf16[1024,384]{1,0:T(8,128)(2,1)S(1)}, u32[]{:S(2)}, u32[]{:S(2)}) collective-permute-start(bf16[1024,384]{1,0:T(8,128)(2,1)S(1)} %copy-done.3), channel_id=1, source_target_pairs={{0,8},{8,16},{16,24},{24,32},{32,40},{40,48},{48,56},{56,64},{64,7... | collective-permute-start | bytes 2359304 | tf_op jit(solution)/shard_map/ppermute | solution.py:20
  127.5 16.8 %collective-permute-start.14 = (bf16[1024,384]{1,0:T(8,128)(2,1)S(1)}, bf16[1024,384]{1,0:T(8,128)(2,1)S(1)}, u32[]{:S(2)}, u32[]{:S(2)}) collective-permute-start(bf16[1024,384]{1,0:T(8,128)(2,1)S(1)} %copy-done.3), channel_id=1, source_target_pairs={{8,0},{16,8},{24,16},{32,24},{40,32},{48,40},{56,48},{64,56},{72,6... | collective-permute-start | bytes 2359304 | tf_op jit(solution)/shard_map/ppermute | solution.py:20
  130.7 27.4 %collective-permute-start.15 = (bf16[1024,384]{1,0:T(8,128)(2,1)S(1)}, bf16[1024,384]{1,0:T(8,128)(2,1)S(1)}, u32[]{:S(2)}, u32[]{:S(2)}) collective-permute-start(bf16[1024,384]{1,0:T(8,128)(2,1)S(1)} %copy-done.3), channel_id=1, source_target_pairs={{16,0},{24,8},{32,16},{40,24},{48,32},{56,40},{64,48},{72,56},{80,... | collective-permute-start | bytes 2359304 | tf_op jit(solution)/shard_map/ppermute | solution.py:20
  (3 other events, 69.4 us)
where the time goes:
time: 164 us; the launch traced here: 163 us
  waiting for transfers between devices  64.2 us (39%)
  starting transfers between devices  45 us (27%)
  blocking collectives  23.7 us (14%)
  local copies, waits for them, and re-layouts  10.2 us (6%)
  matrix products  9.79 us (6%)
  other arithmetic  8.95 us (5%)
    ppermute x16, waiting for transfers between devices, shifted(): lax.ppermute(value, axis, [(source, source + steps) for source in range(f...  64.2 us
    ppermute x16, starting transfers between devices, shifted(): lax.ppermute(value, axis, [(source, source + steps) for source in range(f...  45 us
    psum x1, blocking collectives, body(): lax.psum((squares(video_query), squares(video_key), squares(audio_query),...  23.7 us
    unnamed x39, local copies, waits for them, and re-layouts  8.17 us
    dot_general x6, matrix products, attend_parts(): jnp.dot(rounded, values[:, columns], preferred_element_type=jnp.float32)  5.03 us
    dot_general x6, matrix products, attend_parts(): lax.dot_general(queries[:, columns], key_rows[:, columns], (((1,), (1,)),...  4.76 us
  transfers between devices with their start and end apart: 16, of which 11 were waited for; matrix products, arithmetic and copies ran while one was open for 12% of the time, Pallas kernels for 0%

commit v1 on v0

v1 whole, which is shorter than its diff:
```python
import math

import jax
import jax.numpy as jnp
from jax import lax
from jax.experimental import pallas as pl
from jax.experimental.pallas import tpu as pltpu
from jax.sharding import PartitionSpec as P

MESH = pl.DeviceIdType.MESH
F32 = jnp.float32
BF16 = jnp.bfloat16
E = 128
BLOCK = 128
REACH = 2
EPS = 1e-06
MASKED = -1e30
WINDOW = 2 * REACH + 1
OFFSETS = (-1, 1, -2, 2)
SCORE_SCALE = math.log2(math.e) / math.sqrt(E)
VMEM_LIMIT = 60 * 1024 * 1024


def contract_last(left, right):
    return lax.dot_general(left, right, (((1,), (1,)), ((), ())), preferred_element_type=F32)


def head(ref, h):
    return ref[:, h * E : (h + 1) * E]


def kernel(
    n_video, n_audio,
    vq_hbm, vk_hbm, vv_hbm, aq_hbm, ak_hbm, av_hbm, vqg_hbm, vkg_hbm, aqg_hbm, akg_hbm, pairs_hbm,
    vout_hbm, aout_hbm,
    vq, vk, vv, aq_raw, ak_raw, aq, ak, av, vout, aout, mask,
    sums_a, sums_a_in, sums_v, sums_v_in,
    part_o, part_s, back_o, back_s, mine_o, mine_s,
    vqg, vkg, aqg, akg, pairs,
    load_sem, out_sem, sa_send, sa_recv, sv_send, sv_recv,
    av_send, av_recv, aq_send, aq_recv, ak_send, ak_recv,
    po_send, po_recv, ps_send, ps_recv,
):
    me = lax.axis_index("video")
    mine_z = lax.axis_index("audio")
    width = vq.shape[1] * n_audio
    heads = vq.shape[1] // E
    v_blocks = vq.shape[0] // BLOCK

    def near(offset):
        return (lax.rem(me + offset + n_video, n_video), mine_z)

    def peer(step):
        return (me, lax.rem(mine_z + step, n_audio))

    loads = [
        pltpu.make_async_copy(source, target, load_sem.at[i])
        for i, (source, target) in enumerate(
            (
                (aq_hbm, aq_raw), (ak_hbm, ak_raw), (vk_hbm, vk), (vq_hbm, vq), (pairs_hbm, pairs), (aqg_hbm, aqg),
                (akg_hbm, akg), (vqg_hbm, vqg), (vkg_hbm, vkg), (vv_hbm, vv), (av_hbm, av.at[REACH]),
            )
        )
    ]
    for load in loads:
        load.start()

    barrier = pltpu.get_barrier_semaphore()
    for offset in OFFSETS:
        pl.semaphore_signal(barrier, inc=1, device_id=near(offset), device_id_type=MESH)
    for step in range(1, n_audio):
        pl.semaphore_signal(barrier, inc=1, device_id=peer(step), device_id_type=MESH)

    lane = lax.broadcasted_iota(jnp.int32, (BLOCK, 128), 1)

    def row_sums(ref, block):
        wide = ref[block * BLOCK : (block + 1) * BLOCK, :].astype(F32)
        return jnp.sum(wide * wide, axis=1, keepdims=True)

    loads[0].wait()
    loads[1].wait()
    table = jnp.where(lane == 0, row_sums(aq_raw, 0), 0.0)
    table = jnp.where(lane == 1, row_sums(ak_raw, 0), table)
    sums_a[...] = table.T[:8]

    pl.semaphore_wait(barrier, len(OFFSETS) + n_audio - 1)

    def exchange(source, into, send, recv):
        return [
            pltpu.make_async_remote_copy(
                src_ref=source, dst_ref=into.at[step - 1], send_sem=send.at[step - 1], recv_sem=recv.at[step - 1],
                device_id=peer(step), device_id_type=MESH,
            )
            for step in range(1, n_audio)
        ]

    def spread(source, into, send, recv):
        return [
            pltpu.make_async_remote_copy(
                src_ref=source, dst_ref=into.at[REACH - offset], send_sem=send.at[i], recv_sem=recv.at[REACH - offset],
                device_id=near(offset), device_id_type=MESH,
            )
            for i, offset in enumerate(OFFSETS)
        ]

    def arrived(ref, recv, slot):
        pltpu.make_async_remote_copy(
            src_ref=ref.at[slot], dst_ref=ref.at[slot], send_sem=recv.at[slot], recv_sem=recv.at[slot],
            device_id=near(1), device_id_type=MESH,
        ).wait_recv()

    sa_copies = exchange(sums_a, sums_a_in, sa_send, sa_recv)
    for copy in sa_copies:
        copy.start()
    av_copies = spread(av_hbm, av, av_send, av_recv)
    for copy in av_copies:
        copy.start()

    loads[2].wait()
    loads[3].wait()
    table = jnp.zeros((BLOCK, 128), F32)
    for block in range(v_blocks):
        table = jnp.where(lane == block, row_sums(vk, block), table)
        table = jnp.where(lane == v_blocks + block, row_sums(vq, block), table)
    sums_v[...] = table.T[: 2 * v_blocks]
    sv_copies = exchange(sums_v, sums_v_in, sv_send, sv_recv)
    for copy in sv_copies:
        copy.start()

    for load in loads[4:9]:
        load.wait()
    row_id = lax.broadcasted_iota(jnp.int32, (v_blocks, 128), 0) + me * v_blocks
    lane_id = lax.broadcasted_iota(jnp.int32, (v_blocks, 128), 1)
    low = jnp.full((v_blocks, 128), MASKED, F32)
    for slot in range(WINDOW):
        at, _ = near(slot - REACH)
        for k in range(pairs.shape[0]):
            low = jnp.where((lane_id == slot) & (row_id == pairs[k, at]), 0.0, low)
    low = jnp.where(lane_id < WINDOW, low, 0.0)
    for block in range(v_blocks):
        mask[block * BLOCK : (block + 1) * BLOCK, :] = jnp.broadcast_to(low[block : block + 1], (BLOCK, 128)).astype(BF16)

    def factors(own, arrivals, copies, rows):
        total = own[...]
        for i, copy in enumerate(copies):
            copy.wait_recv()
            total = total + arrivals[i]
        inverse = lax.rsqrt(total / width + EPS)
        return jnp.concatenate([inverse, jnp.zeros((128 - rows, 128), F32)], axis=0).T

    def normalized(block_ref, block, column, gain):
        rows = slice(block * BLOCK, (block + 1) * BLOCK)
        return (block_ref[rows, :].astype(F32) * column * gain).astype(BF16)

    gain_aq = (aqg[...] * SCORE_SCALE)[None, :]
    gain_vq = (vqg[...] * SCORE_SCALE)[None, :]
    gain_ak = akg[...][None, :]
    gain_vk = vkg[...][None, :]

    columns = factors(sums_a, sums_a_in, sa_copies, 8)
    aq[REACH] = normalized(aq_raw, 0, columns[:, 0:1], gain_aq)
    aq_copies = spread(aq.at[REACH], aq, aq_send, aq_recv)
    for copy in aq_copies:
        copy.start()
    ak[REACH] = normalized(ak_raw, 0, columns[:, 1:2], gain_ak)
    ak_copies = spread(ak.at[REACH], ak, ak_send, ak_recv)
    for copy in ak_copies:
        copy.start()

    columns = factors(sums_v, sums_v_in, sv_copies, 2 * v_blocks)
    for block in range(v_blocks):
        rows = slice(block * BLOCK, (block + 1) * BLOCK)
        vk[rows, :] = normalized(vk, block, columns[:, block : block + 1], gain_vk)
    for block in range(v_blocks):
        rows = slice(block * BLOCK, (block + 1) * BLOCK)
        at = v_blocks + block
        vq[rows, :] = normalized(vq, block, columns[:, at : at + 1], gain_vq)

    loads[9].wait()
    loads[10].wait()

    def chosen(slot):
        return jnp.where(lane == slot, 1.0, 0.0).astype(BF16)

    def blend(queries, keys, values):
        scores = contract_last(queries, keys)
        top = jnp.max(scores, axis=1, keepdims=True)
        weights = jnp.exp2(scores - top).astype(BF16)
        ones = jnp.ones(values.shape, BF16)
        mixed = jnp.dot(weights, jnp.concatenate([values, ones], axis=1), preferred_element_type=F32)
        return top, mixed[:, :E], mixed[:, E:]

    def audio_part(slot, into_o, into_s):
        logs = jnp.zeros((BLOCK, 128), F32)
        for h in range(heads):
            queries = jnp.concatenate([head(aq.at[slot], h), chosen(slot)], axis=1)
            keys = jnp.concatenate([head(vk, h), mask[...]], axis=1)
            top, mixed, total = blend(queries, keys, head(vv, h))
            into_o[:, h * E : (h + 1) * E] = (mixed / total).astype(into_o.dtype)
            logs = jnp.where(lane == h, top + jnp.log2(total), logs)
        into_s[...] = logs.T[:8]

    audio_part(REACH, mine_o, mine_s)
    part_copies = []
    for i, offset in enumerate(OFFSETS):
        slot = REACH + offset
        arrived(aq, aq_recv, slot)
        audio_part(slot, part_o.at[i], part_s.at[i])
        for source, into, send, recv in ((part_o, back_o, po_send, po_recv), (part_s, back_s, ps_send, ps_recv)):
            copy = pltpu.make_async_remote_copy(
                src_ref=source.at[i], dst_ref=into.at[REACH - offset], send_sem=send.at[i],
                recv_sem=recv.at[REACH - offset], device_id=near(offset), device_id_type=MESH,
            )
            copy.start()
            part_copies.append(copy)

    for offset in OFFSETS:
        arrived(ak, ak_recv, REACH + offset)
        arrived(av, av_recv, REACH + offset)
    out_copies = []
    for h in range(heads):
        keys = jnp.concatenate(
            [jnp.concatenate([head(ak.at[slot], h), chosen(slot)], axis=1) for slot in range(WINDOW)], axis=0
        )
        values = jnp.concatenate([head(av.at[slot], h) for slot in range(WINDOW)], axis=0)
        queries = jnp.concatenate([head(vq, h), mask[...]], axis=1)
        _, mixed, total = blend(queries, keys, values)
        vout[:, h * E : (h + 1) * E] = mixed / total
        copy = pltpu.make_async_copy(
            vout.at[:, h * E : (h + 1) * E], vout_hbm.at[:, h * E : (h + 1) * E], out_sem.at[h]
        )
        copy.start()
        out_copies.append(copy)

    for offset in OFFSETS:
        arrived(back_o, po_recv, REACH + offset)
        arrived(back_s, ps_recv, REACH + offset)
    slots = [REACH + offset for offset in OFFSETS]
    logs = jnp.concatenate(
        [mine_s[...]] + [back_s[slot] for slot in slots] + [jnp.zeros((128 - 8 * WINDOW, 128), F32)], axis=0
    ).T
    for h in range(heads):
        cols = [logs[:, 8 * i + h : 8 * i + h + 1] for i in range(WINDOW)]
        top = cols[0]
        for col in cols[1:]:
            top = jnp.maximum(top, col)
        scales = [jnp.exp2(col - top) for col in cols]
        total = scales[0]
        for scale in scales[1:]:
            total = total + scale
        mixed = scales[0] * head(mine_o, h)
        for scale, slot in zip(scales[1:], slots):
            mixed = mixed + scale * head(back_o.at[slot], h).astype(F32)
        aout[:, h * E : (h + 1) * E] = mixed / total
    copy = pltpu.make_async_copy(aout, aout_hbm, out_sem.at[heads])
    copy.start()
    out_copies.append(copy)

    for copy in sa_copies + sv_copies + av_copies + aq_copies + ak_copies + part_copies:
        copy.wait_send()
    for copy in out_copies:
        copy.wait()


def solution(mesh):
    n_video, n_audio = mesh.shape["video"], mesh.shape["audio"]

    def body(vq, vk, vv, aq, ak, av, vqg, vkg, aqg, akg, pairs):
        rows_v, wide = vq.shape
        rows_a = aq.shape[0]
        heads = wide // E
        blocks = rows_v // BLOCK
        anywhere = pl.BlockSpec(memory_space=pl.ANY)
        in_hbm = pl.BlockSpec(memory_space=pltpu.HBM)
        dma = pltpu.SemaphoreType.DMA
        near = len(OFFSETS)
        return pl.pallas_call(
            lambda *refs: kernel(n_video, n_audio, *refs),
            out_shape=(
                jax.ShapeDtypeStruct((rows_v, wide), F32),
                jax.ShapeDtypeStruct((rows_a, wide), F32),
            ),
            in_specs=[in_hbm] * 11,
            out_specs=(anywhere, anywhere),
            scratch_shapes=[
                pltpu.VMEM((rows_v, wide), BF16),
                pltpu.VMEM((rows_v, wide), BF16),
                pltpu.VMEM((rows_v, wide), BF16),
                pltpu.VMEM((rows_a, wide), BF16),
                pltpu.VMEM((rows_a, wide), BF16),
                pltpu.VMEM((WINDOW, rows_a, wide), BF16),
                pltpu.VMEM((WINDOW, rows_a, wide), BF16),
                pltpu.VMEM((WINDOW, rows_a, wide), BF16),
                pltpu.VMEM((rows_v, wide), F32),
                pltpu.VMEM((rows_a, wide), F32),
                pltpu.VMEM((rows_v, 128), BF16),
                pltpu.VMEM((8, 128), F32),
                pltpu.VMEM((n_audio - 1, 8, 128), F32),
                pltpu.VMEM((2 * blocks, 128), F32),
                pltpu.VMEM((n_audio - 1, 2 * blocks, 128), F32),
                pltpu.VMEM((near, rows_a, wide), BF16),
                pltpu.VMEM((near, 8, 128), F32),
                pltpu.VMEM((WINDOW, rows_a, wide), BF16),
                pltpu.VMEM((WINDOW, 8, 128), F32),
                pltpu.VMEM((rows_a, wide), F32),
                pltpu.VMEM((8, 128), F32),
                pltpu.VMEM((wide,), F32),
                pltpu.VMEM((wide,), F32),
                pltpu.VMEM((wide,), F32),
                pltpu.VMEM((wide,), F32),
                pltpu.SMEM(pairs.shape[::-1], jnp.int32),
                dma((11,)),
                dma((heads + 1,)),
                dma((n_audio - 1,)),
                dma((n_audio - 1,)),
                dma((n_audio - 1,)),
                dma((n_audio - 1,)),
                dma((near,)),
                dma((WINDOW,)),
                dma((near,)),
                dma((WINDOW,)),
                dma((near,)),
                dma((WINDOW,)),
                dma((near,)),
                dma((WINDOW,)),
                dma((near,)),
                dma((WINDOW,)),
            ],
            compiler_params=pltpu.CompilerParams(
                collective_id=0, has_side_effects=True, vmem_limit_bytes=VMEM_LIMIT
            ),
            name="paired_attention",
        )(vq, vk, vv, aq, ak, av, vqg, vkg, aqg, akg, pairs.T)

    both = P("video", "audio")
    return jax.shard_map(
        body,
        mesh=mesh,
        in_specs=(both,) * 6 + (P("audio"),) * 4 + (P(),),
        out_specs=(both, both),
        check_vma=False,
    )
```

time: 164 us -> 40 us (0.24)
  the two profiles are of different devices: /device:TPU:6 before, /device:TPU:1 now
where the time goes in v1:
time: 40 us; the launch traced here: 39.8 us
  Pallas kernels  35.8 us (89%)
  local copies, waits for them, and re-layouts  3.37 us (8%)
  between operations  0.65 us (2%)
    pallas_call x1, Pallas kernels, body(): pl.pallas_call(lambda *refs: kernel(n_video, n_audio, *refs), out_shape=(...  35.8 us
    unnamed x4, local copies, waits for them, and re-layouts  3.37 us

profile of v1, /device:TPU:1, one launch (start us, length us, event | category | flops | bytes accessed | tf_op | source)
XLA Modules:
  0.0 39.8 jit_solution(1883149189051244356)
XLA Ops:
  0.6 35.8 %paired_attention.1 = (f32[1024,384]{1,0:T(8,128)}, f32[128,384]{1,0:T(8,128)}) custom-call(bf16[1024,384]{1,0:T(8,128)(2,1)} %refs_0_.1, bf16[1024,384]{1,0:T(8,128)(2,1)} %refs_1_.1, bf16[1024,384]{1,0:T(8,128)(2,1)} %refs_2_.1, bf16[128,384]{1,0:T(8,128)(2,1)} %refs_3_.1, bf16[128,384]{1,0:T(8,128)(2,1)} %refs_4_.1, bf16[128,384]{1,0:T(8,128)(2,1)} %refs_5_.1, ...), custom_call_target="tpu_custom_call" | custom-call | tf_op jit(solution)/shard_map/paired_attention/pallas_call | solution.py:277
  36.5 0.0 copy-start
  36.5 2.7 %copy.15 = f32[1024,384]{1,0:T(8,128)} copy(f32[1024,384]{1,0:T(8,128)} %get-tuple-element.4) | data formatting | bytes 3145728
  39.2 0.0 copy-done
  39.2 0.7 %copy.16 = f32[128,384]{1,0:T(8,128)} copy(f32[128,384]{1,0:T(8,128)S(1)} %copy-done) | data formatting | bytes 393216
Async XLA Ops:
  36.5 2.7 %copy-start = (f32[128,384]{1,0:T(8,128)S(1)}, f32[128,384]{1,0:T(8,128)}, u32[]{:S(2)}) copy-start(f32[128,384]{1,0:T(8,128)} %get-tuple-element.5) | copy-start | bytes 589828

commit v2 on v1

v2 whole, which is shorter than its diff:
```python
import math

import jax
import jax.numpy as jnp
from jax import lax
from jax.experimental import pallas as pl
from jax.experimental.pallas import tpu as pltpu
from jax.sharding import PartitionSpec as P

MESH = pl.DeviceIdType.MESH
F32 = jnp.float32
BF16 = jnp.bfloat16
E = 128
BLOCK = 128
EPS = 1e-06
MASKED = -1e30
SCORE_SCALE = math.log2(math.e) / math.sqrt(E)
VMEM_LIMIT = 60 * 1024 * 1024

PLACES = (0, -1, 1, 2, -2)
WINDOW = len(PLACES)
MIRROR = (0, 1, 2, 4, 3)
OTHER, BESIDE, AHEAD, BEHIND = range(1, WINDOW)
STEPS = (1, 2, -1, -2)


def contract_last(left, right):
    return lax.dot_general(left, right, (((1,), (1,)), ((), ())), preferred_element_type=F32)


def head(ref, h):
    return ref[:, h * E : (h + 1) * E]


def kernel(
    n_video, n_audio,
    vq_hbm, vk_hbm, vv_hbm, aq_hbm, ak_hbm, av_hbm, vqg_hbm, vkg_hbm, aqg_hbm, akg_hbm, pairs_hbm,
    vout, aout,
    vq, vk, vv, aq, ak, av, mask, scores_a, scores_v,
    sums_a, sums_a_in, sums_a_on, sums_a_far, sums_v, sums_v_in, sums_v_on, sums_v_far, factors_a,
    part_o, part_s, back_o, back_s, mine_o, mine_s,
    vqg, vkg, aqg, akg, pairs,
    load_sem, sa_send, sa_recv, sa_far_send, sa_far_recv, sv_send, sv_recv, sv_far_send, sv_far_recv, fa_send, fa_recv,
    aq_send, aq_recv, ak_send, ak_recv, av_send, av_recv,
    po_send, po_recv, ps_send, ps_recv,
):
    me = lax.axis_index("video")
    mine_z = lax.axis_index("audio")
    side = 2 * lax.rem(me, 2) - 1
    width = vq.shape[1] * n_audio
    heads = vq.shape[1] // E
    v_blocks = vq.shape[0] // BLOCK

    def at(place):
        return lax.rem(me + PLACES[place] * side + n_video, n_video)

    def near(place):
        return (at(place), mine_z)

    def peer(step):
        return (me, lax.rem(mine_z + step + n_audio, n_audio))

    loads = [
        pltpu.make_async_copy(source, target, load_sem.at[i])
        for i, (source, target) in enumerate(
            (
                (aq_hbm, aq.at[0]), (ak_hbm, ak.at[0]), (vk_hbm, vk), (vq_hbm, vq), (pairs_hbm, pairs), (aqg_hbm, aqg),
                (akg_hbm, akg), (vqg_hbm, vqg), (vkg_hbm, vkg), (vv_hbm, vv), (av_hbm, av.at[0]),
            )
        )
    ]
    loads[0].start()
    loads[1].start()
    barrier = pltpu.get_barrier_semaphore()
    for place in range(1, WINDOW):
        pl.semaphore_signal(barrier, inc=1, device_id=near(place), device_id_type=MESH)
    for step in STEPS:
        pl.semaphore_signal(barrier, inc=1, device_id=peer(step), device_id_type=MESH)
    for load in loads[2:]:
        load.start()

    lane = lax.broadcasted_iota(jnp.int32, (BLOCK, 128), 1)

    def row_sums(rows):
        wide = rows.astype(F32)
        return jnp.sum(wide * wide, axis=1, keepdims=True)

    loads[0].wait()
    loads[1].wait()
    table = jnp.where(lane == 0, row_sums(aq[0]), 0.0)
    table = jnp.where(lane == 1, row_sums(ak[0]), table)
    sums_a[...] = table.T[:2]

    pl.semaphore_wait(barrier, WINDOW - 1 + len(STEPS))

    sent = []

    def push(source, into, slot, send, recv, place):
        copy = pltpu.make_async_remote_copy(
            src_ref=source, dst_ref=into.at[slot], send_sem=send, recv_sem=recv.at[slot],
            device_id=near(place), device_id_type=MESH,
        )
        copy.start()
        sent.append(copy)

    def exchange(source, into, send, recv):
        copies = [
            pltpu.make_async_remote_copy(
                src_ref=source, dst_ref=into.at[STEPS.index(-step)], send_sem=send.at[i], recv_sem=recv.at[STEPS.index(-step)],
                device_id=peer(step), device_id_type=MESH,
            )
            for i, step in enumerate(STEPS)
        ]
        for copy in copies:
            copy.start()
        sent.extend(copies)
        return copies

    def pass_on(arrivals, copies, on, far, send, recv):
        for copy in copies:
            copy.wait_recv()
        on[...] = arrivals[STEPS.index(1)] + arrivals[STEPS.index(2)]
        copies = [
            pltpu.make_async_remote_copy(
                src_ref=source, dst_ref=far.at[i], send_sem=send.at[i], recv_sem=recv.at[i],
                device_id=peer(step), device_id_type=MESH,
            )
            for i, (source, step) in enumerate(((on, -2), (arrivals.at[STEPS.index(-1)], 2)))
        ]
        for copy in copies:
            copy.start()
        sent.extend(copies)
        return copies

    def factors(own, arrivals, far, copies):
        total = own[...]
        for i in range(len(STEPS)):
            total = total + arrivals[i]
        for i, copy in enumerate(copies):
            copy.wait_recv()
            total = total + far[i]
        return lax.rsqrt(total / width + EPS)

    def spread(source, into, send, recv):
        for i, place in enumerate((AHEAD, BEHIND, OTHER)):
            push(source, into, MIRROR[place], send.at[i], recv, place)

    def arrived(ref, recv, slot):
        pltpu.make_async_remote_copy(
            src_ref=ref.at[slot], dst_ref=ref.at[slot], send_sem=recv.at[slot], recv_sem=recv.at[slot],
            device_id=near(OTHER), device_id_type=MESH,
        ).wait_recv()

    def relay(ref, send, recv):
        arrived(ref, recv, BEHIND)
        push(ref.at[BEHIND], ref, BESIDE, send.at[3], recv, OTHER)

    sa_copies = exchange(sums_a, sums_a_in, sa_send, sa_recv)
    spread(aq_hbm, aq, aq_send, aq_recv)
    spread(ak_hbm, ak, ak_send, ak_recv)
    spread(av_hbm, av, av_send, av_recv)

    loads[2].wait()
    loads[3].wait()
    table = jnp.zeros((BLOCK, 128), F32)
    for block in range(v_blocks):
        rows = slice(block * BLOCK, (block + 1) * BLOCK)
        table = jnp.where(lane == block, row_sums(vk[rows, :]), table)
        table = jnp.where(lane == v_blocks + block, row_sums(vq[rows, :]), table)
    sums_v[...] = table.T[: 2 * v_blocks]
    sv_copies = exchange(sums_v, sums_v_in, sv_send, sv_recv)

    for load in loads[4:]:
        load.wait()
    row_id = lax.broadcasted_iota(jnp.int32, (v_blocks, 128), 0) + me * v_blocks
    lane_id = lax.broadcasted_iota(jnp.int32, (v_blocks, 128), 1)
    low = jnp.full((v_blocks, 128), MASKED, F32)
    for place in range(WINDOW):
        where = at(place)
        for k in range(pairs.shape[0]):
            low = jnp.where((lane_id == place) & (row_id == pairs[k, where]), 0.0, low)
    low = jnp.where(lane_id < WINDOW, low, 0.0)
    for block in range(v_blocks):
        mask[block * BLOCK : (block + 1) * BLOCK, :] = jnp.broadcast_to(low[block : block + 1], (BLOCK, 128)).astype(BF16)

    gain_a = (aqg[...] * vkg[...] * SCORE_SCALE)[None, :]
    gain_v = (vqg[...] * akg[...] * SCORE_SCALE)[None, :]
    vq[...] = (vq[...].astype(F32) * gain_v).astype(BF16)

    def chosen(place):
        return jnp.where(lane == place, 1.0, 0.0).astype(BF16)

    def marked(rows, place):
        return jnp.concatenate([rows, chosen(place)], axis=1)

    def span(places):
        return slice(places[0] * BLOCK, (places[-1] + 1) * BLOCK)

    def audio_scores(places):
        for h in range(heads):
            queries = jnp.concatenate(
                [marked((head(aq.at[place], h).astype(F32) * head(gain_a, h)).astype(BF16), place) for place in places], axis=0
            )
            keys = jnp.concatenate([head(vk, h), mask[...]], axis=1)
            scores_a[h, span(places), :] = contract_last(queries, keys)

    def video_scores(places):
        for h in range(heads):
            keys = jnp.concatenate([marked(head(ak.at[place], h), place) for place in places], axis=0)
            queries = jnp.concatenate([head(vq, h), mask[...]], axis=1)
            scores_v[h, :, span(places)] = contract_last(queries, keys)

    def blend(scores, key_scale, query_scale, values):
        scores = scores * key_scale
        top = jnp.max(scores, axis=1, keepdims=True)
        weights = jnp.exp2((scores - top) * query_scale).astype(BF16)
        ones = jnp.ones(values.shape, BF16)
        mixed = jnp.dot(weights, jnp.concatenate([values, ones], axis=1), preferred_element_type=F32)
        return top * query_scale, mixed[:, :E], mixed[:, E:]

    def as_columns(pieces):
        rows = sum(piece.shape[0] for piece in pieces)
        return jnp.concatenate(list(pieces) + [jnp.zeros((128 - rows, 128), F32)], axis=0).T

    sa_copies = pass_on(sums_a_in, sa_copies, sums_a_on, sums_a_far, sa_far_send, sa_far_recv)
    audio_scores((0,))
    video_scores((0,))
    relay(aq, aq_send, aq_recv)
    sv_copies = pass_on(sums_v_in, sv_copies, sums_v_on, sums_v_far, sv_far_send, sv_far_recv)
    factors_a[0] = factors(sums_a, sums_a_in, sums_a_far, sa_copies)
    for place in (AHEAD, BEHIND, BESIDE, OTHER):
        push(factors_a.at[0], factors_a, MIRROR[place], fa_send.at[place - 1], fa_recv, place)

    arrived(aq, aq_recv, AHEAD)
    audio_scores((AHEAD, BEHIND))
    arrived(ak, ak_recv, AHEAD)
    relay(ak, ak_send, ak_recv)
    for place in (OTHER, BESIDE):
        arrived(aq, aq_recv, place)
    audio_scores((OTHER, BESIDE))
    video_scores((AHEAD, BEHIND))
    relay(av, av_send, av_recv)

    factors_v = factors(sums_v, sums_v_in, sums_v_far, sv_copies)
    scale_k = jnp.concatenate([factors_v[block : block + 1] for block in range(v_blocks)], axis=1)

    def audio_part(places):
        columns = as_columns([factors_a[place] for place in places])
        query_scale = jnp.concatenate([columns[:, 2 * i : 2 * i + 1] for i in range(len(places))], axis=0)
        logs = [jnp.zeros((BLOCK, 128), F32) for _ in places]
        for h in range(heads):
            top, mixed, total = blend(scores_a[h, span(places), :], scale_k, query_scale, head(vv, h))
            result = mixed / total
            log = top + jnp.log2(total)
            for i, place in enumerate(places):
                rows = slice(i * BLOCK, (i + 1) * BLOCK)
                logs[i] = jnp.where(lane == h, log[rows], logs[i])
                if place == 0:
                    mine_o[h] = result[rows]
                else:
                    part_o[place - 1, h] = result[rows].astype(BF16)
        for i, place in enumerate(places):
            if place == 0:
                mine_s[...] = logs[i].T[:8]
            else:
                part_s[place - 1] = logs[i].T[:8]
                push(part_o.at[place - 1], back_o, MIRROR[place], po_send.at[place - 1], po_recv, place)
                push(part_s.at[place - 1], back_s, MIRROR[place], ps_send.at[place - 1], ps_recv, place)

    audio_part((0,))
    arrived(factors_a, fa_recv, AHEAD)
    arrived(factors_a, fa_recv, BEHIND)
    audio_part((AHEAD, BEHIND))
    arrived(factors_a, fa_recv, OTHER)
    arrived(factors_a, fa_recv, BESIDE)
    audio_part((OTHER, BESIDE))

    for place in (OTHER, BESIDE):
        arrived(ak, ak_recv, place)
    video_scores((OTHER, BESIDE))
    for place in (OTHER, AHEAD, BESIDE):
        arrived(av, av_recv, place)
    scale_a = jnp.concatenate([factors_a[place, 1:2] for place in range(WINDOW)], axis=1)
    columns_v = as_columns([factors_v[v_blocks:]])
    query_scale = jnp.concatenate([columns_v[:, block : block + 1] for block in range(v_blocks)], axis=0)
    for h in range(heads):
        values = jnp.concatenate([head(av.at[place], h) for place in range(WINDOW)], axis=0)
        _, mixed, total = blend(scores_v[h], scale_a, query_scale, values)
        vout[:, h * E : (h + 1) * E] = mixed / total

    for place in range(1, WINDOW):
        arrived(back_s, ps_recv, place)
        arrived(back_o, po_recv, place)
    logs = as_columns([mine_s[...]] + [back_s[place] for place in range(1, WINDOW)])
    for h in range(heads):
        cols = [logs[:, 8 * i + h : 8 * i + h + 1] for i in range(WINDOW)]
        top = cols[0]
        for col in cols[1:]:
            top = jnp.maximum(top, col)
        scales = [jnp.exp2(col - top) for col in cols]
        total = scales[0]
        for scale in scales[1:]:
            total = total + scale
        mixed = scales[0] * mine_o[h]
        for place in range(1, WINDOW):
            mixed = mixed + scales[place] * back_o[place, h].astype(F32)
        aout[:, h * E : (h + 1) * E] = mixed / total

    for copy in sent:
        copy.wait_send()


def solution(mesh):
    n_video, n_audio = mesh.shape["video"], mesh.shape["audio"]

    def body(vq, vk, vv, aq, ak, av, vqg, vkg, aqg, akg, pairs):
        rows_v, wide = vq.shape
        rows_a = aq.shape[0]
        blocks = rows_v // BLOCK
        heads = wide // E
        in_hbm = pl.BlockSpec(memory_space=pltpu.HBM)
        in_vmem = pl.BlockSpec(memory_space=pltpu.VMEM)
        dma = pltpu.SemaphoreType.DMA
        near = WINDOW - 1
        return pl.pallas_call(
            lambda *refs: kernel(n_video, n_audio, *refs),
            out_shape=(pltpu.VMEM((rows_v, wide), F32), pltpu.VMEM((rows_a, wide), F32)),
            in_specs=[in_hbm] * 11,
            out_specs=(in_vmem, in_vmem),
            scratch_shapes=[
                pltpu.VMEM((rows_v, wide), BF16),
                pltpu.VMEM((rows_v, wide), BF16),
                pltpu.VMEM((rows_v, wide), BF16),
                pltpu.VMEM((WINDOW, rows_a, wide), BF16),
                pltpu.VMEM((WINDOW, rows_a, wide), BF16),
                pltpu.VMEM((WINDOW, rows_a, wide), BF16),
                pltpu.VMEM((rows_v, 128), BF16),
                pltpu.VMEM((heads, WINDOW * rows_a, rows_v), F32),
                pltpu.VMEM((heads, rows_v, WINDOW * rows_a), F32),
                pltpu.VMEM((2, 128), F32),
                pltpu.VMEM((len(STEPS), 2, 128), F32),
                pltpu.VMEM((2, 128), F32),
                pltpu.VMEM((2, 2, 128), F32),
                pltpu.VMEM((2 * blocks, 128), F32),
                pltpu.VMEM((len(STEPS), 2 * blocks, 128), F32),
                pltpu.VMEM((2 * blocks, 128), F32),
                pltpu.VMEM((2, 2 * blocks, 128), F32),
                pltpu.VMEM((WINDOW, 2, 128), F32),
                pltpu.VMEM((near, heads, rows_a, E), BF16),
                pltpu.VMEM((near, 8, 128), F32),
                pltpu.VMEM((WINDOW, heads, rows_a, E), BF16),
                pltpu.VMEM((WINDOW, 8, 128), F32),
                pltpu.VMEM((heads, rows_a, E), F32),
                pltpu.VMEM((8, 128), F32),
                pltpu.VMEM((wide,), F32),
                pltpu.VMEM((wide,), F32),
                pltpu.VMEM((wide,), F32),
                pltpu.VMEM((wide,), F32),
                pltpu.SMEM(pairs.shape[::-1], jnp.int32),
                dma((11,)),
                dma((len(STEPS),)),
                dma((len(STEPS),)),
                dma((2,)),
                dma((2,)),
                dma((len(STEPS),)),
                dma((len(STEPS),)),
                dma((2,)),
                dma((2,)),
                dma((near,)),
                dma((WINDOW,)),
                dma((near,)),
                dma((WINDOW,)),
                dma((near,)),
                dma((WINDOW,)),
                dma((near,)),
                dma((WINDOW,)),
                dma((near,)),
                dma((WINDOW,)),
                dma((near,)),
                dma((WINDOW,)),
            ],
            compiler_params=pltpu.CompilerParams(
                collective_id=0, has_side_effects=True, vmem_limit_bytes=VMEM_LIMIT
            ),
            name="paired_attention",
        )(vq, vk, vv, aq, ak, av, vqg, vkg, aqg, akg, pairs.T)

    both = P("video", "audio")
    return jax.shard_map(
        body,
        mesh=mesh,
        in_specs=(both,) * 6 + (P("audio"),) * 4 + (P(),),
        out_specs=(both, both),
        check_vma=False,
    )
```

time: 40 us -> 34.5 us (0.86)
  the two profiles are of different devices: /device:TPU:1 before, /device:TPU:64 now
where the time goes in v2:
time: 34.5 us; the launch traced here: 34.3 us
  Pallas kernels  31.9 us (92%)
  local copies, waits for them, and re-layouts  1.82 us (5%)
  between operations  0.64 us (2%)
    pallas_call x1, Pallas kernels, body(): pl.pallas_call(lambda *refs: kernel(n_video, n_audio, *refs), out_shape=(...  31.9 us
    unnamed x2, local copies, waits for them, and re-layouts  1.82 us

profile of v2, /device:TPU:64, one launch (start us, length us, event | category | flops | bytes accessed | tf_op | source)
XLA Modules:
  0.0 34.3 jit_solution(6888624458417503138)
XLA Ops:
  0.6 31.9 %paired_attention.1 = (f32[1024,384]{1,0:T(8,128)S(1)}, f32[128,384]{1,0:T(8,128)S(1)}) custom-call(bf16[1024,384]{1,0:T(8,128)(2,1)} %refs_0_.1, bf16[1024,384]{1,0:T(8,128)(2,1)} %refs_1_.1, bf16[1024,384]{1,0:T(8,128)(2,1)} %refs_2_.1, bf16[128,384]{1,0:T(8,128)(2,1)} %refs_3_.1, bf16[128,384]{1,0:T(8,128)(2,1)} %refs_4_.1, bf16[128,384]{1,0:T(8,128)(2,1)} %refs_5_.1, ...), custom_call_target="tpu_custom_call" | custom-call | tf_op jit(solution)/shard_map/paired_attention/pallas_call | solution.py:325
  32.5 1.1 %copy.15 = f32[1024,384]{1,0:T(8,128)} copy(f32[1024,384]{1,0:T(8,128)S(1)} %get-tuple-element.2) | data formatting | bytes 3145728
  33.7 0.7 %copy.16 = f32[128,384]{1,0:T(8,128)} copy(f32[128,384]{1,0:T(8,128)S(1)} %get-tuple-element.3) | data formatting | bytes 393216

commit v3 on v2

--- a/solution.py
+++ b/solution.py
@@ -210,9 +210,7 @@
             queries = jnp.concatenate([head(vq, h), mask[...]], axis=1)
             scores_v[h, :, span(places)] = contract_last(queries, keys)
 
-    def blend(scores, key_scale, query_scale, values):
-        scores = scores * key_scale
-        top = jnp.max(scores, axis=1, keepdims=True)
+    def blend(scores, top, query_scale, values):
         weights = jnp.exp2((scores - top) * query_scale).astype(BF16)
         ones = jnp.ones(values.shape, BF16)
         mixed = jnp.dot(weights, jnp.concatenate([values, ones], axis=1), preferred_element_type=F32)
@@ -239,17 +237,24 @@
         arrived(aq, aq_recv, place)
     audio_scores((OTHER, BESIDE))
     video_scores((AHEAD, BEHIND))
-    relay(av, av_send, av_recv)
 
     factors_v = factors(sums_v, sums_v_in, sums_v_far, sv_copies)
     scale_k = jnp.concatenate([factors_v[block : block + 1] for block in range(v_blocks)], axis=1)
 
-    def audio_part(places):
+    def audio_tops(places):
+        tops = []
+        for h in range(heads):
+            scaled = scores_a[h, span(places), :] * scale_k
+            scores_a[h, span(places), :] = scaled
+            tops.append(jnp.max(scaled, axis=1, keepdims=True))
+        return tops
+
+    def audio_part(places, tops):
         columns = as_columns([factors_a[place] for place in places])
         query_scale = jnp.concatenate([columns[:, 2 * i : 2 * i + 1] for i in range(len(places))], axis=0)
         logs = [jnp.zeros((BLOCK, 128), F32) for _ in places]
         for h in range(heads):
-            top, mixed, total = blend(scores_a[h, span(places), :], scale_k, query_scale, head(vv, h))
+            top, mixed, total = blend(scores_a[h, span(places), :], tops[h], query_scale, head(vv, h))
             result = mixed / total
             log = top + jnp.log2(total)
             for i, place in enumerate(places):
@@ -267,13 +272,16 @@
                 push(part_o.at[place - 1], back_o, MIRROR[place], po_send.at[place - 1], po_recv, place)
                 push(part_s.at[place - 1], back_s, MIRROR[place], ps_send.at[place - 1], ps_recv, place)
 
-    audio_part((0,))
+    audio_part((0,), audio_tops((0,)))
+    tops_far = audio_tops((AHEAD, BEHIND))
+    tops_near = audio_tops((OTHER, BESIDE))
+    relay(av, av_send, av_recv)
     arrived(factors_a, fa_recv, AHEAD)
     arrived(factors_a, fa_recv, BEHIND)
-    audio_part((AHEAD, BEHIND))
+    audio_part((AHEAD, BEHIND), tops_far)
     arrived(factors_a, fa_recv, OTHER)
     arrived(factors_a, fa_recv, BESIDE)
-    audio_part((OTHER, BESIDE))
+    audio_part((OTHER, BESIDE), tops_near)
 
     for place in (OTHER, BESIDE):
         arrived(ak, ak_recv, place)
@@ -285,7 +293,8 @@
     query_scale = jnp.concatenate([columns_v[:, block : block + 1] for block in range(v_blocks)], axis=0)
     for h in range(heads):
         values = jnp.concatenate([head(av.at[place], h) for place in range(WINDOW)], axis=0)
-        _, mixed, total = blend(scores_v[h], scale_a, query_scale, values)
+        scaled = scores_v[h] * scale_a
+        _, mixed, total = blend(scaled, jnp.max(scaled, axis=1, keepdims=True), query_scale, values)
         vout[:, h * E : (h + 1) * E] = mixed / total
 
     for place in range(1, WINDOW):

time: 34.5 us -> 34.3 us (level)
  no operation moved by 1% of the time
where the time goes in v3:
time: 34.3 us; the launch traced here: 34.2 us
  Pallas kernels  31.7 us (92%)
  local copies, waits for them, and re-layouts  1.82 us (5%)
  between operations  0.64 us (2%)
    pallas_call x1, Pallas kernels, body(): pl.pallas_call(lambda *refs: kernel(n_video, n_audio, *refs), out_shape=(...  31.7 us
    unnamed x2, local copies, waits for them, and re-layouts  1.82 us

profile of v3, /device:TPU:64, one launch (start us, length us, event | category | flops | bytes accessed | tf_op | source)
XLA Modules:
  0.0 34.2 jit_solution(8132732584815317111)
XLA Ops:
  0.6 31.7 %paired_attention.1 = (f32[1024,384]{1,0:T(8,128)S(1)}, f32[128,384]{1,0:T(8,128)S(1)}) custom-call(bf16[1024,384]{1,0:T(8,128)(2,1)} %refs_0_.1, bf16[1024,384]{1,0:T(8,128)(2,1)} %refs_1_.1, bf16[1024,384]{1,0:T(8,128)(2,1)} %refs_2_.1, bf16[128,384]{1,0:T(8,128)(2,1)} %refs_3_.1, bf16[128,384]{1,0:T(8,128)(2,1)} %refs_4_.1, bf16[128,384]{1,0:T(8,128)(2,1)} %refs_5_.1, ...), custom_call_target="tpu_custom_call" | custom-call | tf_op jit(solution)/shard_map/paired_attention/pallas_call | solution.py:334
  32.3 1.1 %copy.15 = f32[1024,384]{1,0:T(8,128)} copy(f32[1024,384]{1,0:T(8,128)S(1)} %get-tuple-element.2) | data formatting | bytes 3145728
  33.5 0.7 %copy.16 = f32[128,384]{1,0:T(8,128)} copy(f32[128,384]{1,0:T(8,128)S(1)} %get-tuple-element.3) | data formatting | bytes 393216

commit v4 on v3

--- a/solution.py
+++ b/solution.py
@@ -22,6 +22,7 @@
 MIRROR = (0, 1, 2, 4, 3)
 OTHER, BESIDE, AHEAD, BEHIND = range(1, WINDOW)
 STEPS = (1, 2, -1, -2)
+PARTS = 2
 
 
 def contract_last(left, right):
@@ -293,9 +294,11 @@
     query_scale = jnp.concatenate([columns_v[:, block : block + 1] for block in range(v_blocks)], axis=0)
     for h in range(heads):
         values = jnp.concatenate([head(av.at[place], h) for place in range(WINDOW)], axis=0)
-        scaled = scores_v[h] * scale_a
-        _, mixed, total = blend(scaled, jnp.max(scaled, axis=1, keepdims=True), query_scale, values)
-        vout[:, h * E : (h + 1) * E] = mixed / total
+        for part in range(PARTS):
+            rows = slice(part * vq.shape[0] // PARTS, (part + 1) * vq.shape[0] // PARTS)
+            scaled = scores_v[h, rows, :] * scale_a
+            _, mixed, total = blend(scaled, jnp.max(scaled, axis=1, keepdims=True), query_scale[rows], values)
+            vout[rows, h * E : (h + 1) * E] = mixed / total
 
     for place in range(1, WINDOW):
         arrived(back_s, ps_recv, place)

time: 34.3 us -> 34.3 us (level)
  no operation moved by 1% of the time
where the time goes in v4:
time: 34.3 us; the launch traced here: 34.2 us
  Pallas kernels  31.7 us (92%)
  local copies, waits for them, and re-layouts  1.82 us (5%)
  between operations  0.64 us (2%)
    pallas_call x1, Pallas kernels, body(): pl.pallas_call(lambda *refs: kernel(n_video, n_audio, *refs), out_shape=(...  31.7 us
    unnamed x2, local copies, waits for them, and re-layouts  1.82 us

profile of v4, /device:TPU:64, one launch (start us, length us, event | category | flops | bytes accessed | tf_op | source)
XLA Modules:
  0.0 34.2 jit_solution(11734384758468123410)
XLA Ops:
  0.6 31.7 %paired_attention.1 = (f32[1024,384]{1,0:T(8,128)S(1)}, f32[128,384]{1,0:T(8,128)S(1)}) custom-call(bf16[1024,384]{1,0:T(8,128)(2,1)} %refs_0_.1, bf16[1024,384]{1,0:T(8,128)(2,1)} %refs_1_.1, bf16[1024,384]{1,0:T(8,128)(2,1)} %refs_2_.1, bf16[128,384]{1,0:T(8,128)(2,1)} %refs_3_.1, bf16[128,384]{1,0:T(8,128)(2,1)} %refs_4_.1, bf16[128,384]{1,0:T(8,128)(2,1)} %refs_5_.1, ...), custom_call_target="tpu_custom_call" | custom-call | tf_op jit(solution)/shard_map/paired_attention/pallas_call | solution.py:337
  32.3 1.1 %copy.15 = f32[1024,384]{1,0:T(8,128)} copy(f32[1024,384]{1,0:T(8,128)S(1)} %get-tuple-element.2) | data formatting | bytes 3145728
  33.5 0.7 %copy.16 = f32[128,384]{1,0:T(8,128)} copy(f32[128,384]{1,0:T(8,128)S(1)} %get-tuple-element.3) | data formatting | bytes 393216
